TPU v7x, 512 devices: a whole 4x4x16 slice. The times are simulated.
512 devices in a mesh: group: 16 (over x, y_lo, core), head: 32 (over z, y_hi).
Axes of the slice: x: 4, y: 4 (y_hi: 2, y_lo: 2; y = y_hi * 2 + y_lo), z: 16, core: 2. Of those that a mesh axis runs over, the one named last changes fastest.
Arguments:
- enc_resid: bfloat16 [1024, 1024], P('group'), may hold values from -6 to 6
- enc_qkv: bfloat16 [3, 1024, 16384], P(None, 'group', 'head'), may hold values from -6 to 6
- enc_bias: float32 [64, 64], replicated, may hold values from -4 to 315
- out_weight: bfloat16 [16384, 1024], P(('head', 'group')), may hold values from -0.046875 to 0.046875
- final_gain: float32 [1024], replicated, may hold values from 0.25 to 1.75
- key_weight: bfloat16 [1024, 16384], P('group', 'head'), may hold values from -0.1875 to 0.1875
- value_weight: bfloat16 [1024, 16384], P('group', 'head'), may hold values from -0.1875 to 0.1875
- dec_query: bfloat16 [6144, 16384], P('group', 'head'), may hold values from -6 to 6
- cross_bias: float32 [384, 64], replicated, may hold values from -4 to 315
- out_grad: bfloat16 [6144, 16384], P('group', 'head'), may hold values from -6 to 6
- sources: int32 [16, 3], replicated, may hold values from 0 to 15, all different within a row
- head_keep: int32 [16, 128], P('group', 'head'), may hold values 0 or 1
Outputs:
- context: bfloat16 [6144, 16384], P('group', 'head')
- memory_grad: bfloat16 [1024, 1024], P('group')
Inputs may be any that keep to these rules, and one draw needn't show every extreme that they name: `sources`: each row names 3 different encoder groups; every encoder group is named by some row.
All inputs are finite; a program needn't handle non-finite values. No bound on the sum of `head_keep` on one device may be relied on, other than what follows from the above.
Results may differ from a plain program's by a relative error of at most 0.034.
Values may be sent and summed in bfloat16 or wider, within the bound.
A program may use at most 64 MiB of HBM per device.

v0:
```python
import math
import jax
import jax.numpy as jnp
from jax import lax
from jax.sharding import PartitionSpec as P

DK = 128
SEQ = 64
QROWS = 384
MEM = 3


def softmax_rows(scores):
    top = jnp.max(scores, axis=-1, keepdims=True)
    expd = jnp.exp(scores - top)
    return expd / jnp.sum(expd, axis=-1, keepdims=True)


def norm_rows(memory, gain):
    inv = lax.rsqrt(jnp.mean(memory * memory, axis=-1, keepdims=True) + 1e-06)
    return (memory * inv * gain).astype(jnp.bfloat16)


def norm_grad(memory, upstream, gain):
    inv = lax.rsqrt(jnp.mean(memory * memory, axis=-1, keepdims=True) + 1e-06)
    normed = memory * inv
    scaled = upstream * gain
    return (inv * (scaled - normed * jnp.mean(scaled * normed, axis=-1, keepdims=True))).astype(
        jnp.bfloat16
    )


def times_transposed(left, weight):
    return lax.dot_general(
        left, weight, (((1,), (1,)), ((), ())), preferred_element_type=jnp.float32
    )


def shards(
    enc_resid,
    enc_qkv,
    enc_bias,
    out_weight,
    final_gain,
    key_weight,
    value_weight,
    dec_query,
    cross_bias,
    out_grad,
    sources,
    head_keep,
):
    scale = 1.0 / math.sqrt(DK)
    width = enc_qkv.shape[2]
    nheads = width // DK
    mine = lax.axis_index("group")
    enc_q = enc_qkv[0].reshape(SEQ, nheads, DK)
    enc_k = enc_qkv[1].reshape(SEQ, nheads, DK)
    enc_v = enc_qkv[2].reshape(SEQ, nheads, DK)
    enc_scores = (
        jnp.einsum("qhd,khd->hqk", enc_q, enc_k, preferred_element_type=jnp.float32) * scale
        + enc_bias
    )
    enc_prob = softmax_rows(enc_scores).astype(jnp.bfloat16)
    enc_ctx = jnp.einsum("hqk,khd->qhd", enc_prob, enc_v, preferred_element_type=jnp.float32)
    enc_ctx = enc_ctx.astype(jnp.bfloat16).reshape(SEQ, width)
    partial_out = jnp.dot(
        enc_ctx,
        lax.all_gather(out_weight, "group", axis=0, tiled=True),
        preferred_element_type=jnp.float32,
    )
    key_full, value_full = (
        lax.all_gather(key_weight, "group", axis=0, tiled=True),
        lax.all_gather(value_weight, "group", axis=0, tiled=True),
    )
    memory = enc_resid.astype(jnp.float32) + lax.psum(partial_out, "head")
    mem_norm = norm_rows(memory, final_gain)
    keys = jnp.dot(mem_norm, key_full, preferred_element_type=jnp.float32).astype(jnp.bfloat16)
    values = jnp.dot(mem_norm, value_full, preferred_element_type=jnp.float32).astype(jnp.bfloat16)
    paired = jnp.concatenate([keys, values], axis=1)
    my_sources = lax.dynamic_index_in_dim(sources, mine, 0, keepdims=False)
    every_pair = lax.all_gather(paired, "group", axis=0, tiled=True)
    chosen = jnp.concatenate(
        [
            lax.dynamic_slice_in_dim(every_pair, my_sources[slot] * SEQ, SEQ, 0)
            for slot in range(MEM)
        ],
        axis=0,
    )
    mem_keys = chosen[:, :width].reshape(MEM * SEQ, nheads, DK)
    mem_values = chosen[:, width:].reshape(MEM * SEQ, nheads, DK)
    query = dec_query.reshape(QROWS, nheads, DK)
    keep_low = head_keep[0].astype(jnp.bfloat16)
    bias_all = jnp.tile(cross_bias, (1, MEM))
    cross = (
        jnp.einsum("qhd,khd->hqk", query, mem_keys, preferred_element_type=jnp.float32) * scale
        + bias_all
    )
    prob = softmax_rows(cross)
    prob_low = prob.astype(jnp.bfloat16)
    attn = jnp.einsum("hqk,khd->qhd", prob_low, mem_values, preferred_element_type=jnp.float32)
    context = (
        (attn * keep_low.astype(jnp.float32)[None, :, None])
        .astype(jnp.bfloat16)
        .reshape(QROWS, width)
    )
    grad = out_grad.reshape(QROWS, nheads, DK) * keep_low[None, :, None]
    dprob = jnp.einsum("qhd,khd->hqk", grad, mem_values, preferred_element_type=jnp.float32)
    delta = jnp.sum(prob * dprob, axis=-1, keepdims=True)
    dscore = (prob * (dprob - delta) * scale).astype(jnp.bfloat16)
    dk_part = jnp.einsum("hqk,qhd->khd", dscore, query, preferred_element_type=jnp.float32).astype(
        jnp.bfloat16
    )
    dv_part = jnp.einsum("hqk,qhd->khd", prob_low, grad, preferred_element_type=jnp.float32).astype(
        jnp.bfloat16
    )
    dpair = jnp.concatenate(
        [dk_part.reshape(MEM, SEQ, width), dv_part.reshape(MEM, SEQ, width)], axis=2
    )
    flat_sources = sources.reshape(-1)
    picked = (flat_sources == mine).astype(jnp.float32)
    summed = jnp.einsum(
        "m,mrc->rc", picked, lax.all_gather(dpair, "group", axis=0, tiled=True).astype(jnp.float32)
    )
    summed = summed.astype(jnp.bfloat16)
    dnorm_part = times_transposed(summed[:, :width], key_full) + times_transposed(
        summed[:, width:], value_full
    )
    dnorm = lax.psum(dnorm_part.astype(jnp.bfloat16), "head").astype(jnp.float32)
    memory_grad = norm_grad(memory, dnorm, final_gain)
    return (context, memory_grad)


def solution(mesh):
    in_specs = (
        P("group", None),
        P(None, "group", "head"),
        P(),
        P(("head", "group"), None),
        P(),
        P("group", "head"),
        P("group", "head"),
        P("group", "head"),
        P(),
        P("group", "head"),
        P(),
        P("group", "head"),
    )
    out_specs = (P("group", "head"), P("group", None))
    return jax.shard_map(shards, mesh=mesh, in_specs=in_specs, out_specs=out_specs, check_vma=False)
```

profile of v0, /device:TPU:2, one launch (start us, length us, event | category | flops | bytes accessed | tf_op | source)
XLA Modules:
  0.0 869.8 jit_solution(4122692869663150683)
XLA Ops:
  8.0 0.8 copy.42
  8.8 0.9 fusion.64
  10.3 44.2 %all-gather.6.cloned.1.call-done = bf16[512,1024]{1,0:T(8,128)(2,1)} async-done(((bf16[32,1024]{1,0:T(8,128)(2,1)}), bf16[512,1024]{1,0:T(8,128)(2,1)}) %all-gather.6.cloned.1.call-update) | async-done | bytes 1048592 | tf_op jit(solution)/shard_map/all_gather | solution.py:69
  54.4 2.2 fusion.41
  58.0 306.3 %all-reduce.3.cloned.1.call-done = f32[64,1024]{1,0:T(8,128)} async-done(((f32[64,1024]{1,0:T(8,128)}), f32[64,1024]{1,0:T(8,128)}) %all-reduce.3.cloned.1.call-update) | async-done | bytes 262160 | tf_op jit(solution)/shard_map/psum | solution.py:76
  364.3 1.1 multiply_reduce_fusion.2
  365.4 1.0 multiply_convert_fusion.1
  366.5 35.7 %all-gather.10.cloned.1.call-done = bf16[1024,512]{1,0:T(8,128)(2,1)} async-done(((bf16[64,512]{1,0:T(8,128)(2,1)}), bf16[1024,512]{1,0:T(8,128)(2,1)}) %all-gather.10.cloned.1.call-update) | async-done | bytes 1048592 | tf_op jit(solution)/shard_map/all_gather | solution.py:74
  402.2 1.5 convolution_convert_fusion.1
  403.8 41.0 %all-gather.8.cloned.1.call-done = bf16[1024,512]{1,0:T(8,128)(2,1)} async-done(((bf16[64,512]{1,0:T(8,128)(2,1)}), bf16[1024,512]{1,0:T(8,128)(2,1)}) %all-gather.8.cloned.1.call-update) | async-done | bytes 1048592 | tf_op jit(solution)/shard_map/all_gather | solution.py:73
  444.7 1.5 convolution_convert_fusion.2
  449.7 39.5 %all-gather.12.cloned.1.call-done = bf16[1024,1024]{1,0:T(8,128)(2,1)} async-done(((bf16[64,1024]{1,0:T(8,128)(2,1)}), bf16[1024,1024]{1,0:T(8,128)(2,1)}) %all-gather.12.cloned.1.call-update) | async-done | bytes 2097168 | tf_op jit(solution)/shard_map/all_gather | solution.py:82
  489.2 1.1 constant_dynamic-slice_fusion.2
  492.6 2.2 fusion.19
  495.0 0.8 pad_maximum_fusion.1
  496.3 50.1 %all-gather.14.cloned.1.call-done = bf16[48,64,1024]{2,1,0:T(8,128)(2,1)} async-done(((bf16[3,64,1024]{2,1,0:T(8,128)(2,1)}), bf16[48,64,1024]{2,1,0:T(8,128)(2,1)}) %all-gather.14.cloned.1.call-update) | async-done | bytes 6291472 | tf_op jit(solution)/shard_map/all_gather | solution.py:123
  546.4 9.5 %fusion.3 = bf16[1,64,1024]{2,0,1:T(2,128)(2,1)S(1)} fusion(pred[48,1,1]{0,1,2:T(4,128)(4,1)S(1)} %reshape.86, bf16[48,64,1024]{2,1,0:T(8,128)(2,1)} %all-gather.14.cloned.1.call-done), kind=kOutput, calls=%fused_computation.3 | convolution fusion | flops 6291456 | bytes 6422576 | tf_op jit(solution)/shard_map/m,mrc->rc/dot_general | solution.py:122
  556.4 0.7 copy-done.2
  557.2 1.1 fusion.18
  558.3 1.7 fusion.14
  560.0 0.9 copy.55
  560.9 299.3 %all-reduce.5.cloned.1.call-done = bf16[64,1024]{1,0:T(8,128)(2,1)} async-done(((bf16[64,1024]{1,0:T(8,128)(2,1)}), bf16[64,1024]{1,0:T(8,128)(2,1)}) %all-reduce.5.cloned.1.call-update) | async-done | bytes 131088 | tf_op jit(solution)/shard_map/psum | solution.py:129
  860.2 1.1 multiply_reduce_fusion.1
  861.3 1.7 multiply_convert_fusion
  (62 shorter events, 7.5 us)
Async XLA Ops:
  7.2 483.2 %copy-start = (bf16[384,512]{1,0:T(8,128)(2,1)S(1)}, bf16[384,512]{1,0:T(8,128)(2,1)}, u32[]{:S(2)}) copy-start(bf16[384,512]{1,0:T(8,128)(2,1)} %param.19) | copy-start | bytes 1179652
  7.2 47.3 %all-gather.6.cloned.1.call-start = ((), (), s32[]{:S(2)}) async-start(), calls=%async_computation | async-start | bytes 1114112 | tf_op jit(solution)/shard_map/all_gather | solution.py:69
  7.9 356.4 %all-reduce.3.cloned.1.call-start = ((), (), s32[]{:S(2)}) async-start(), calls=%async_computation.1 | async-start | bytes 524288 | tf_op jit(solution)/shard_map/psum | solution.py:76
  10.0 354.3 %copy-start.4 = (bf16[64,1024]{1,0:T(8,128)(2,1)S(1)}, bf16[64,1024]{1,0:T(8,128)(2,1)}, u32[]{:S(2)}) copy-start(bf16[64,1024]{1,0:T(8,128)(2,1)} %param.12) | copy-start | bytes 393220
  10.3 355.2 %copy-start.7 = (f32[1024]{0:T(1024)S(1)}, f32[1024]{0:T(1024)}, u32[]{:S(2)}) copy-start(f32[1024]{0:T(1024)} %param.16) | copy-start | bytes 12292
  56.7 345.6 %all-gather.10.cloned.1.call-start = ((), (), s32[]{:S(2)}) async-start(), calls=%async_computation.3 | async-start | bytes 1114112 | tf_op jit(solution)/shard_map/all_gather | solution.py:74
  57.4 387.3 %all-gather.8.cloned.1.call-start = ((), (), s32[]{:S(2)}) async-start(), calls=%async_computation.2 | async-start | bytes 1114112 | tf_op jit(solution)/shard_map/all_gather | solution.py:73
  58.0 431.2 %all-gather.12.cloned.1.call-start = ((), (), s32[]{:S(2)}) async-start(), calls=%async_computation.4 | async-start | bytes 2228224 | tf_op jit(solution)/shard_map/all_gather | solution.py:82
  366.5 80.5 %copy-start.8 = (s32[16,3]{0,1:T(4,128)S(1)}, s32[16,3]{0,1:T(4,128)}, u32[]{:S(2)}) copy-start(s32[16,3]{0,1:T(4,128)} %param.22) | copy-start | bytes 580
  366.5 83.1 %copy-start.9 = (s32[1,4]{1,0:T(1,128)S(1)}, s32[1,4]{1,0:T(1,128)}, u32[]{:S(2)}) copy-start(s32[1,4]{1,0:T(1,128)} %param.23) | copy-start | bytes 52
  446.9 99.4 %all-gather.14.cloned.1.call-start = ((), (), s32[]{:S(2)}) async-start(), calls=%async_computation.5 | async-start | bytes 6684672 | tf_op jit(solution)/shard_map/all_gather | solution.py:123
  449.7 40.7 %copy-start.6 = (f32[384,64]{0,1:T(8,128)S(1)}, f32[384,64]{0,1:T(8,128)}, u32[]{:S(2)}) copy-start(f32[384,64]{0,1:T(8,128)} %param.20) | copy-start | bytes 294916
  490.4 1.0 copy-start.5
  490.9 1.0 copy-start.10
  495.8 364.3 %all-reduce.5.cloned.1.call-start = ((), (), s32[]{:S(2)}) async-start(), calls=%async_computation.6 | async-start | bytes 262144 | tf_op jit(solution)/shard_map/psum | solution.py:129
  496.3 59.7 %copy-start.3 = (bf16[1024,512]{1,0:T(8,128)(2,1)S(1)}, bf16[1024,512]{1,0:T(8,128)(2,1)}, u32[]{:S(2)}) copy-start(bf16[1024,512]{1,0:T(8,128)(2,1)} %all-gather.8.cloned.1.call-done) | copy-start | bytes 3145732
  555.9 1.2 copy-start.2
  558.3 301.9 %copy-start.1 = (f32[64,1024]{1,0:T(8,128)S(1)}, f32[64,1024]{1,0:T(8,128)}, u32[]{:S(2)}) copy-start(f32[64,1024]{1,0:T(8,128)} %all-reduce.3.cloned.1.call-done) | copy-start | bytes 786436
Sparse Core Ops, SparseCore 0:
  10.2 44.2 all-gather.5
  57.9 306.3 all-reduce.2
  366.7 35.4 all-gather.9
  404.5 40.2 all-gather.7
  447.5 41.6 all-gather.11
  495.9 50.3 all-gather.13
  558.4 301.7 all-reduce.4
where the time goes:
time: 870 us
  waiting for transfers between devices  818 us (94%)
  matrix products  21.8 us (3%)
  between operations  16.4 us (2%)
    psum x1, waiting for transfers between devices, shards(): memory = enc_resid.astype(jnp.float32) + lax.psum(partial_out, 'head')  306 us
    psum x1, waiting for transfers between devices, shards(): lax.psum(dnorm_part.astype(jnp.bfloat16), 'head').astype(jnp.float32)  299 us
    all_gather x1, waiting for transfers between devices, shards(): lax.all_gather(dpair, 'group', axis=0, tiled=True).astype(jnp.float32)  50.1 us
    all_gather x1, waiting for transfers between devices, shards(): lax.all_gather(out_weight, 'group', axis=0, tiled=True)  44.2 us
    all_gather x1, waiting for transfers between devices, shards(): lax.all_gather(key_weight, 'group', axis=0, tiled=True)  41 us
    all_gather x1, waiting for transfers between devices, shards(): every_pair = lax.all_gather(paired, 'group', axis=0, tiled=True)  39.5 us
    all_gather x1, waiting for transfers between devices, shards(): lax.all_gather(value_weight, 'group', axis=0, tiled=True)  35.7 us
  transfers between devices with their start and end apart: 7, of which 7 were waited for; matrix products, arithmetic and copies ran while one was open for 1% of the time, Pallas kernels for 0%

commit v1 on v0

--- a/solution.py
+++ b/solution.py
@@ -126,7 +126,9 @@
     dnorm_part = times_transposed(summed[:, :width], key_full) + times_transposed(
         summed[:, width:], value_full
     )
-    dnorm = lax.psum(dnorm_part.astype(jnp.bfloat16), "head").astype(jnp.float32)
+    dnorm = jnp.sum(lax.all_gather(dnorm_part.astype(jnp.bfloat16), "head"), axis=0).astype(
+        jnp.float32
+    )
     memory_grad = norm_grad(memory, dnorm, final_gain)
     return (context, memory_grad)
 

time: 870 us -> 735 us (0.84)
  the two profiles are of different devices: /device:TPU:2 before, /device:TPU:32 now
where the time goes in v1:
time: 735 us
  waiting for transfers between devices  681 us (93%)
  matrix products  21.8 us (3%)
  between operations  16.4 us (2%)
  other arithmetic  7.85 us (1%)
    psum x1, waiting for transfers between devices, shards(): memory = enc_resid.astype(jnp.float32) + lax.psum(partial_out, 'head')  304 us
    all_gather x1, waiting for transfers between devices, shards(): lax.all_gather(dnorm_part.astype(jnp.bfloat16), 'head')  163 us
    all_gather x1, waiting for transfers between devices, shards(): lax.all_gather(dpair, 'group', axis=0, tiled=True).astype(jnp.float32)  49.8 us
    all_gather x1, waiting for transfers between devices, shards(): lax.all_gather(out_weight, 'group', axis=0, tiled=True)  44.1 us
    all_gather x1, waiting for transfers between devices, shards(): lax.all_gather(key_weight, 'group', axis=0, tiled=True)  41 us
    all_gather x1, waiting for transfers between devices, shards(): every_pair = lax.all_gather(paired, 'group', axis=0, tiled=True)  39.7 us
    all_gather x1, waiting for transfers between devices, shards(): lax.all_gather(value_weight, 'group', axis=0, tiled=True)  37.6 us
  transfers between devices with their start and end apart: 7, of which 7 were waited for; matrix products, arithmetic and copies ran while one was open for 1% of the time, Pallas kernels for 0%

profile of v1, /device:TPU:32, one launch (start us, length us, event | category | flops | bytes accessed | tf_op | source)
XLA Modules:
  0.0 734.6 jit_solution(5716585260843729603)
XLA Ops:
  8.0 0.8 copy.42
  8.8 0.9 fusion.64
  10.3 44.1 %all-gather.8.cloned.1.call-done = bf16[512,1024]{1,0:T(8,128)(2,1)} async-done(((bf16[32,1024]{1,0:T(8,128)(2,1)}), bf16[512,1024]{1,0:T(8,128)(2,1)}) %all-gather.8.cloned.1.call-update) | async-done | bytes 1048592 | tf_op jit(solution)/shard_map/all_gather | solution.py:69
  54.4 2.2 fusion.41
  58.0 304.4 %all-reduce.2.cloned.1.call-done = f32[64,1024]{1,0:T(8,128)} async-done(((f32[64,1024]{1,0:T(8,128)}), f32[64,1024]{1,0:T(8,128)}) %all-reduce.2.cloned.1.call-update) | async-done | bytes 262160 | tf_op jit(solution)/shard_map/psum | solution.py:76
  362.4 1.1 multiply_reduce_fusion.2
  363.5 1.0 multiply_convert_fusion.1
  364.6 37.6 %all-gather.12.cloned.1.call-done = bf16[1024,512]{1,0:T(8,128)(2,1)} async-done(((bf16[64,512]{1,0:T(8,128)(2,1)}), bf16[1024,512]{1,0:T(8,128)(2,1)}) %all-gather.12.cloned.1.call-update) | async-done | bytes 1048592 | tf_op jit(solution)/shard_map/all_gather | solution.py:74
  402.2 1.5 convolution_convert_fusion.1
  403.7 41.0 %all-gather.10.cloned.1.call-done = bf16[1024,512]{1,0:T(8,128)(2,1)} async-done(((bf16[64,512]{1,0:T(8,128)(2,1)}), bf16[1024,512]{1,0:T(8,128)(2,1)}) %all-gather.10.cloned.1.call-update) | async-done | bytes 1048592 | tf_op jit(solution)/shard_map/all_gather | solution.py:73
  444.7 1.5 convolution_convert_fusion.2
  449.6 39.7 %all-gather.14.cloned.1.call-done = bf16[1024,1024]{1,0:T(8,128)(2,1)} async-done(((bf16[64,1024]{1,0:T(8,128)(2,1)}), bf16[1024,1024]{1,0:T(8,128)(2,1)}) %all-gather.14.cloned.1.call-update) | async-done | bytes 2097168 | tf_op jit(solution)/shard_map/all_gather | solution.py:82
  489.3 1.1 constant_dynamic-slice_fusion.2
  492.7 2.2 fusion.19
  495.1 0.8 pad_maximum_fusion.1
  496.4 49.8 %all-gather.16.cloned.1.call-done = bf16[48,64,1024]{2,1,0:T(8,128)(2,1)} async-done(((bf16[3,64,1024]{2,1,0:T(8,128)(2,1)}), bf16[48,64,1024]{2,1,0:T(8,128)(2,1)}) %all-gather.16.cloned.1.call-update) | async-done | bytes 6291472 | tf_op jit(solution)/shard_map/all_gather | solution.py:123
  546.2 9.5 %fusion.3 = bf16[1,64,1024]{2,0,1:T(2,128)(2,1)S(1)} fusion(pred[48,1,1]{0,1,2:T(4,128)(4,1)S(1)} %reshape.87, bf16[48,64,1024]{2,1,0:T(8,128)(2,1)} %all-gather.16.cloned.1.call-done), kind=kOutput, calls=%fused_computation.3 | convolution fusion | flops 6291456 | bytes 6422576 | tf_op jit(solution)/shard_map/m,mrc->rc/dot_general | solution.py:122
  556.2 0.7 copy-done.2
  557.0 1.1 fusion.18
  558.1 1.6 fusion.14
  559.7 0.9 copy.55
  560.6 162.9 %all-gather.18.cloned.1.call-done = bf16[2048,1024]{1,0:T(8,128)(2,1)} async-done(((bf16[64,1024]{1,0:T(8,128)(2,1)}), bf16[2048,1024]{1,0:T(8,128)(2,1)}) %all-gather.18.cloned.1.call-update) | async-done | bytes 4194320 | tf_op jit(solution)/shard_map/all_gather | solution.py:129
  723.6 3.2 reduce_sum.65
  727.0 0.8 multiply_convert_fusion
  (63 shorter events, 7.7 us)
Async XLA Ops:
  7.2 483.3 %copy-start = (bf16[384,512]{1,0:T(8,128)(2,1)S(1)}, bf16[384,512]{1,0:T(8,128)(2,1)}, u32[]{:S(2)}) copy-start(bf16[384,512]{1,0:T(8,128)(2,1)} %param.19) | copy-start | bytes 1179652
  7.2 47.2 %all-gather.8.cloned.1.call-start = ((), (), s32[]{:S(2)}) async-start(), calls=%async_computation | async-start | bytes 1114112 | tf_op jit(solution)/shard_map/all_gather | solution.py:69
  7.9 354.5 %all-reduce.2.cloned.1.call-start = ((), (), s32[]{:S(2)}) async-start(), calls=%async_computation.1 | async-start | bytes 524288 | tf_op jit(solution)/shard_map/psum | solution.py:76
  10.0 352.4 %copy-start.4 = (bf16[64,1024]{1,0:T(8,128)(2,1)S(1)}, bf16[64,1024]{1,0:T(8,128)(2,1)}, u32[]{:S(2)}) copy-start(bf16[64,1024]{1,0:T(8,128)(2,1)} %param.12) | copy-start | bytes 393220
  10.3 353.3 %copy-start.7 = (f32[1024]{0:T(1024)S(1)}, f32[1024]{0:T(1024)}, u32[]{:S(2)}) copy-start(f32[1024]{0:T(1024)} %param.16) | copy-start | bytes 12292
  56.6 345.6 %all-gather.12.cloned.1.call-start = ((), (), s32[]{:S(2)}) async-start(), calls=%async_computation.3 | async-start | bytes 1114112 | tf_op jit(solution)/shard_map/all_gather | solution.py:74
  57.4 387.3 %all-gather.10.cloned.1.call-start = ((), (), s32[]{:S(2)}) async-start(), calls=%async_computation.2 | async-start | bytes 1114112 | tf_op jit(solution)/shard_map/all_gather | solution.py:73
  57.9 431.4 %all-gather.14.cloned.1.call-start = ((), (), s32[]{:S(2)}) async-start(), calls=%async_computation.4 | async-start | bytes 2228224 | tf_op jit(solution)/shard_map/all_gather | solution.py:82
  364.6 82.3 %copy-start.8 = (s32[16,3]{0,1:T(4,128)S(1)}, s32[16,3]{0,1:T(4,128)}, u32[]{:S(2)}) copy-start(s32[16,3]{0,1:T(4,128)} %param.22) | copy-start | bytes 580
  364.6 85.0 %copy-start.9 = (s32[1,4]{1,0:T(1,128)S(1)}, s32[1,4]{1,0:T(1,128)}, u32[]{:S(2)}) copy-start(s32[1,4]{1,0:T(1,128)} %param.23) | copy-start | bytes 52
  446.9 99.3 %all-gather.16.cloned.1.call-start = ((), (), s32[]{:S(2)}) async-start(), calls=%async_computation.5 | async-start | bytes 6684672 | tf_op jit(solution)/shard_map/all_gather | solution.py:123
  449.6 40.9 %copy-start.6 = (f32[384,64]{0,1:T(8,128)S(1)}, f32[384,64]{0,1:T(8,128)}, u32[]{:S(2)}) copy-start(f32[384,64]{0,1:T(8,128)} %param.20) | copy-start | bytes 294916
  490.5 1.0 copy-start.5
  491.0 1.0 copy-start.10
  495.9 227.6 %all-gather.18.cloned.1.call-start = ((), (), s32[]{:S(2)}) async-start(), calls=%async_computation.6 | async-start | bytes 4325376 | tf_op jit(solution)/shard_map/all_gather | solution.py:129
  496.4 59.4 %copy-start.3 = (bf16[1024,512]{1,0:T(8,128)(2,1)S(1)}, bf16[1024,512]{1,0:T(8,128)(2,1)}, u32[]{:S(2)}) copy-start(bf16[1024,512]{1,0:T(8,128)(2,1)} %all-gather.10.cloned.1.call-done) | copy-start | bytes 3145732
  555.7 1.2 copy-start.2
  723.6 3.2 copy-start.1
Sparse Core Ops, SparseCore 0:
  10.2 44.1 all-gather.7
  57.8 304.5 all-reduce.1
  364.8 37.3 all-gather.11
  404.4 40.2 all-gather.9
  447.4 41.8 all-gather.13
  496.1 50.0 all-gather.15
  558.2 165.3 all-gather.17
